TPU v7x, 256 devices: a whole 4x4x8 slice. The times are simulated.
256 devices in a mesh: leaf: 16 (over z, core), front: 16 (over x, y).
Axes of the slice: x: 4, y: 4, z: 8, core: 2. Of those that a mesh axis runs over, the one named last changes fastest.
Arguments:
- rhs_leaf: float32 [16, 1024, 256], P('leaf', 'front'), may hold values from -6 to 6
- rhs_top: float32 [15, 1024, 256], P(None, 'front'), may hold values from -6 to 6
- inv_leaf: bfloat16 [16, 1024, 1024], P('leaf', 'front'), as said below
- inv_top: bfloat16 [15, 1024, 1024], P(None, 'front'), as said below
- off_leaf: bfloat16 [16, 1024, 1024], P('leaf', None, 'front'), may hold values from -0.09375 to 0.09375
- off_top: bfloat16 [14, 1024, 1024], P(None, None, 'front'), may hold values from -0.09375 to 0.09375
- idx_leaf: int32 [16, 1024], P('leaf'), may hold values from 0 to 4095, as said below
- idx_top: int32 [14, 1024], replicated, may hold values from 0 to 3071, as said below
Outputs:
- leaf_solution: float32 [16, 1024, 256], P('leaf', 'front')
- ancestor_solution: float32 [16, 4, 1024, 256], P('leaf', None, 'front')
Inputs may be any that keep to these rules, and one draw needn't show every extreme that they name: `idx_leaf`: entry r of row g is a * 1024 + q with a < 4: update row r of split-level front g lands on row q of its depth-a ancestor. `idx_top`: row j belongs to the upper front with heap number h = j + 2; its entries are a * 1024 + q with a < floor(log2 h): update row r lands on row q of h's depth-a ancestor. `inv_leaf`: every block is lower triangular with a positive diagonal. `inv_top`: every block is lower triangular with a positive diagonal.
All inputs are finite; a program needn't handle non-finite values.
Results may differ from a plain program's by a relative error of at most 0.0055.
Values may be sent and summed in bfloat16 or wider, within the bound.
No kernel may reach another device: no remote copies, remote signals or barrier semaphores. Data moves between devices by JAX's collectives and lax.ppermute only.
A program may use at most 64 MiB of HBM per device.

v0:
```python
import jax
import jax.numpy as jnp
from jax import lax
from jax.sharding import PartitionSpec as P


def partner(block, axis, stride):
    count = lax.axis_size(axis)
    route = []
    for low in range(count):
        high = low | 1 << stride
        if high != low and high < count:
            route += [(low, high), (high, low)]
    return lax.ppermute(block, axis, route)


def local(rhs_leaf, rhs_top, inv_leaf, inv_top, off_leaf, off_top, idx_leaf, idx_top):
    front_width = inv_leaf.shape[2]
    rhs_count = rhs_leaf.shape[2]
    leaves = lax.axis_size("leaf")
    depth_count = leaves.bit_length() - 1
    leaf_pos = lax.axis_index("leaf")

    def apply_inverse(inverse, right_side):
        rounded = right_side.astype(jnp.bfloat16)
        return jnp.dot(
            inverse,
            lax.all_gather(rounded, "front", axis=0, tiled=True),
            preferred_element_type=jnp.float32,
        )

    def spread(off_block, solution, row_list, count):
        partial_value = jnp.dot(
            off_block, solution.astype(jnp.bfloat16), preferred_element_type=jnp.float32
        )
        dense_rows = jax.ops.segment_sum(partial_value, row_list, num_segments=count * front_width)
        dense_rows = dense_rows.reshape(count, front_width, rhs_count)
        return lax.psum_scatter(dense_rows, "front", scatter_dimension=1, tiled=True)

    leaf_solution = apply_inverse(inv_leaf[0], rhs_leaf[0])
    pending = spread(off_leaf[0], leaf_solution, idx_leaf[0], depth_count)
    solved = []
    for section_num in range(depth_count):
        pending = pending + partner(pending, "leaf", section_num)
        heap_node = jnp.right_shift(leaves + leaf_pos, section_num + 1)
        right_side = (
            lax.dynamic_index_in_dim(rhs_top, heap_node - 1, 0, keepdims=False) - pending[0]
        )
        inverse = lax.dynamic_index_in_dim(inv_top, heap_node - 1, 0, keepdims=False)
        solution = apply_inverse(inverse, right_side)
        solved.append(solution)
        if section_num + 1 < depth_count:
            off_block = lax.dynamic_index_in_dim(off_top, heap_node - 2, 0, keepdims=False)
            row_list = lax.dynamic_index_in_dim(idx_top, heap_node - 2, 0, keepdims=False)
            pending = pending[1:] + spread(
                off_block, solution, row_list, depth_count - section_num - 1
            )
    return (leaf_solution[None], jnp.stack(solved)[None])


def solution(mesh):
    placed = (
        P("leaf", "front", None),
        P(None, "front", None),
        P("leaf", "front", None),
        P(None, "front", None),
        P("leaf", None, "front"),
        P(None, None, "front"),
        P("leaf", None),
        P(),
    )
    return jax.shard_map(
        local,
        mesh=mesh,
        in_specs=placed,
        out_specs=(P("leaf", "front", None), P("leaf", None, "front", None)),
        check_vma=False,
    )
```

profile of v0, /device:TPU:32, one launch (start us, length us, event | category | flops | bytes accessed | tf_op | source)
XLA Modules:
  0.0 521.0 jit_solution(1386196292948095497)
XLA Ops:
  7.2 0.0 copy-start
  7.2 0.0 reduce-scatter.5.cloned.1.call-start
  7.2 1.0 convert_element_type.42
  8.2 24.3 %all-gather = bf16[1,1024,256]{2,1,0:T(8,128)(2,1)S(1)} all-gather(bf16[1,64,256]{2,1,0:T(8,128)(2,1)S(1)} %convert_element_type.42), channel_id=2, replica_groups=mesh['leaf'=16,'front'=16] {'front'}, dimensions={1}, use_global_device_ids=true | all-gather | bytes 557056 | tf_op jit(solution)/shard_map/all_gather | solution.py:28
  32.5 1.1 fusion.13
  33.6 0.0 copy-start.1
  33.6 1.2 convolution_bitcast_fusion
  34.8 1.3 copy.10
  36.1 8.7 %scatter_custom_fusion = f32[4096,256]{1,0:T(8,128)} fusion(s32[1024]{0:T(1024)} %bitcast.71, f32[1024,256]{1,0:T(8,128)} %copy.10, f32[]{:T(128)} %constant.69.clone.1), kind=kCustom, calls=%fused_computation.4 | custom fusion | flops 262144 | bytes 4194816 | tf_op jit(solution)/shard_map/scatter-add | solution.py:36
  44.8 0.0 copy-done.1
  44.8 0.0 reduce-scatter.5.cloned.1.call-update
  44.8 0.0 reduce-scatter.7.cloned.1.call-start
  44.9 83.3 %reduce-scatter.5.cloned.1.call-done = f32[4,64,256]{2,1,0:T(8,128)} async-done(((f32[4,1024,256]{2,1,0:T(8,128)}), f32[4,64,256]{2,1,0:T(8,128)}) %reduce-scatter.5.cloned.1.call-update) | async-done | bytes 262160 | tf_op jit(solution)/shard_map/reduce_scatter | solution.py:38
  128.2 0.0 collective-permute-start
  128.2 0.9 constant_dynamic-slice_fusion.2
  129.1 0.9 collective-permute-done
  129.9 1.0 add.98
  130.9 0.9 fusion.38
  131.8 23.3 %all-gather.1 = bf16[1,1024,256]{2,1,0:T(8,128)(2,1)S(1)} all-gather(bf16[1,64,256]{2,1,0:T(8,128)(2,1)S(1)} %fusion.38), channel_id=3, replica_groups=mesh['leaf'=16,'front'=16] {'front'}, dimensions={1}, use_global_device_ids=true | all-gather | bytes 557056 | tf_op jit(solution)/shard_map/all_gather | solution.py:28
  155.0 0.0 copy-done
  155.0 0.2 fusion.11
  155.2 1.2 fusion.23
  156.5 7.9 %scatter_custom_fusion.1 = f32[3072,256]{1,0:T(8,128)} fusion(s32[1024]{0:T(1024)S(1)} %bitcast.70, f32[1024,256]{1,0:T(8,128)S(1)} %fusion.23, f32[]{:T(128)} %constant.69.clone.1), kind=kCustom, calls=%fused_computation.6 | custom fusion | flops 262144 | bytes 3145732 | tf_op jit(solution)/shard_map/scatter-add | solution.py:36
  164.4 0.0 reduce-scatter.7.cloned.1.call-update
  164.4 0.0 reduce-scatter.9.cloned.1.call-start
  164.4 79.7 %reduce-scatter.7.cloned.1.call-done = f32[3,64,256]{2,1,0:T(8,128)} async-done(((f32[3,1024,256]{2,1,0:T(8,128)}), f32[3,64,256]{2,1,0:T(8,128)}) %reduce-scatter.7.cloned.1.call-update) | async-done | bytes 196624 | tf_op jit(solution)/shard_map/reduce_scatter | solution.py:38
  244.1 0.9 slice_add_fusion
  245.1 0.6 collective-permute-start.1
  245.6 5.2 collective-permute-done.1
  250.9 0.9 fusion.37
  251.7 23.5 %all-gather.2 = bf16[1,1024,256]{2,1,0:T(8,128)(2,1)S(1)} all-gather(bf16[1,64,256]{2,1,0:T(8,128)(2,1)S(1)} %fusion.37), channel_id=4, replica_groups=mesh['leaf'=16,'front'=16] {'front'}, dimensions={1}, use_global_device_ids=true | all-gather | bytes 557056 | tf_op jit(solution)/shard_map/all_gather | solution.py:28
  275.2 0.2 fusion.9
  275.4 1.2 fusion.20
  276.7 7.5 %scatter_custom_fusion.2 = f32[2048,256]{1,0:T(8,128)} fusion(s32[1024]{0:T(1024)S(1)} %bitcast.69, f32[1024,256]{1,0:T(8,128)S(1)} %fusion.20, f32[]{:T(128)} %constant.69.clone.1), kind=kCustom, calls=%fused_computation.10 | custom fusion | flops 262144 | bytes 2097156 | tf_op jit(solution)/shard_map/scatter-add | solution.py:36
  284.1 0.0 reduce-scatter.9.cloned.1.call-update
  284.2 0.0 reduce-scatter.11.cloned.1.call-start
  284.2 78.2 %reduce-scatter.9.cloned.1.call-done = f32[2,64,256]{2,1,0:T(8,128)} async-done(((f32[2,1024,256]{2,1,0:T(8,128)}), f32[2,64,256]{2,1,0:T(8,128)}) %reduce-scatter.9.cloned.1.call-update) | async-done | bytes 131088 | tf_op jit(solution)/shard_map/reduce_scatter | solution.py:38
  362.4 0.9 slice_add_fusion.1
  363.3 2.6 collective-permute-start.2
  365.9 3.8 collective-permute-done.2
  369.8 0.9 fusion.36
  370.6 23.2 %all-gather.3 = bf16[1,1024,256]{2,1,0:T(8,128)(2,1)S(1)} all-gather(bf16[1,64,256]{2,1,0:T(8,128)(2,1)S(1)} %fusion.36), channel_id=5, replica_groups=mesh['leaf'=16,'front'=16] {'front'}, dimensions={1}, use_global_device_ids=true | all-gather | bytes 557056 | tf_op jit(solution)/shard_map/all_gather | solution.py:28
  393.9 0.2 fusion.7
  394.1 1.2 fusion.17
  395.3 7.1 %scatter_custom_fusion.3 = f32[1024,256]{1,0:T(8,128)} fusion(s32[1024]{0:T(1024)S(1)} %bitcast.68, f32[1024,256]{1,0:T(8,128)S(1)} %fusion.17, f32[]{:T(128)} %constant.69.clone.1), kind=kCustom, calls=%fused_computation.21 | custom fusion | flops 262144 | bytes 1048580 | tf_op jit(solution)/shard_map/scatter-add | solution.py:36
  402.4 0.0 reduce-scatter.11.cloned.1.call-update
  402.4 77.7 %reduce-scatter.11.cloned.1.call-done = f32[1,64,256]{2,1,0:T(8,128)} async-done(((f32[1,1024,256]{2,1,0:T(8,128)}), f32[1,64,256]{2,1,0:T(8,128)}) %reduce-scatter.11.cloned.1.call-update) | async-done | bytes 65552 | tf_op jit(solution)/shard_map/reduce_scatter | solution.py:38
  480.1 0.8 slice_add_fusion.2
  480.9 5.0 collective-permute-start.3
  485.9 3.4 collective-permute-done.3
  489.3 0.9 subtract_convert_fusion
  490.2 23.3 %all-gather.4 = bf16[1,1024,256]{2,1,0:T(8,128)(2,1)S(1)} all-gather(bf16[1,64,256]{2,1,0:T(8,128)(2,1)S(1)} %subtract_convert_fusion), channel_id=6, replica_groups=mesh['leaf'=16,'front'=16] {'front'}, dimensions={1}, use_global_device_ids=true | all-gather | bytes 557056 | tf_op jit(solution)/shard_map/all_gather | solution.py:28
  513.5 0.2 convolution_bitcast_fusion.1
  513.7 0.7 maximum_bitcast_fusion
  (2 shorter events, 0.0 us)
Async XLA Ops:
  7.2 147.9 %copy-start = (bf16[15,64,1024]{2,1,0:T(8,128)(2,1)S(1)}, bf16[15,64,1024]{2,1,0:T(8,128)(2,1)}, u32[]{:S(2)}) copy-start(bf16[15,64,1024]{2,1,0:T(8,128)(2,1)} %param.11) | copy-start | bytes 5898244
  7.2 121.0 %reduce-scatter.5.cloned.1.call-start = ((), (), s32[]{:S(2)}) async-start(), calls=%async_computation.4 | async-start | bytes 4456448 | tf_op jit(solution)/shard_map/reduce_scatter | solution.py:38
  33.6 11.2 %copy-start.1 = (f32[64,256]{1,0:T(8,128)}, f32[64,256]{1,0:T(8,128)S(1)}, u32[]{:S(2)}) copy-start(f32[64,256]{1,0:T(8,128)S(1)} %fusion.13) | copy-start | bytes 196612
  44.8 199.3 %reduce-scatter.7.cloned.1.call-start = ((), (), s32[]{:S(2)}) async-start(), calls=%async_computation.5 | async-start | bytes 3342336 | tf_op jit(solution)/shard_map/reduce_scatter | solution.py:38
  128.2 1.7 collective-permute-start
  164.4 198.0 %reduce-scatter.9.cloned.1.call-start = ((), (), s32[]{:S(2)}) async-start(), calls=%async_computation.6 | async-start | bytes 2228224 | tf_op jit(solution)/shard_map/reduce_scatter | solution.py:38
  245.1 5.8 %collective-permute-start.1 = (f32[3,64,256]{2,1,0:T(8,128)S(1)}, f32[3,64,256]{2,1,0:T(8,128)S(1)}, u32[]{:S(2)}, u32[]{:S(2)}) collective-permute-start(f32[3,64,256]{2,1,0:T(8,128)S(1)} %slice_add_fusion), channel_id=1, source_target_pairs={{0,32},{32,0},{16,48},{48,16},{64,96},{96,64},{80,112},{112,80},{1... | collective-permute-start | bytes 589832 | tf_op jit(solution)/shard_map/ppermute | solution.py:14
  284.2 195.9 %reduce-scatter.11.cloned.1.call-start = ((), (), s32[]{:S(2)}) async-start(), calls=%async_computation.7 | async-start | bytes 1114112 | tf_op jit(solution)/shard_map/reduce_scatter | solution.py:38
  363.3 6.5 %collective-permute-start.2 = (f32[2,64,256]{2,1,0:T(8,128)S(1)}, f32[2,64,256]{2,1,0:T(8,128)S(1)}, u32[]{:S(2)}, u32[]{:S(2)}) collective-permute-start(f32[2,64,256]{2,1,0:T(8,128)S(1)} %slice_add_fusion.1), channel_id=1, source_target_pairs={{0,64},{64,0},{16,80},{80,16},{32,96},{96,32},{48,112},{112,48},{1... | collective-permute-start | bytes 393224 | tf_op jit(solution)/shard_map/ppermute | solution.py:14
  480.9 8.4 %collective-permute-start.3 = (f32[1,64,256]{2,1,0:T(8,128)S(1)}, f32[1,64,256]{2,1,0:T(8,128)S(1)}, u32[]{:S(2)}, u32[]{:S(2)}) collective-permute-start(f32[1,64,256]{2,1,0:T(8,128)S(1)} %slice_add_fusion.2), channel_id=1, source_target_pairs={{0,128},{128,0},{16,144},{144,16},{32,160},{160,32},{48,176},{176,... | collective-permute-start | bytes 196616 | tf_op jit(solution)/shard_map/ppermute | solution.py:14
Sparse Core Ops, SparseCore 0:
  45.0 83.1 reduce-scatter.4
  164.5 79.5 reduce-scatter.6
  284.3 78.0 reduce-scatter.8
  402.5 77.5 reduce-scatter.10
where the time goes:
time: 522 us; the launch traced here: 521 us
  waiting for transfers between devices  332 us (64%)
  blocking collectives  118 us (23%)
  other arithmetic  39.9 us (8%)
  between operations  13.9 us (3%)
  starting transfers between devices  8.32 us (2%)
  matrix products  6.91 us (1%)
    reduce_scatter x4, waiting for transfers between devices, spread(): lax.psum_scatter(dense_rows, 'front', scatter_dimension=1, tiled=True)  319 us
    all_gather x5, blocking collectives, apply_inverse(): lax.all_gather(rounded, 'front', axis=0, tiled=True)  118 us
    scatter-add x4, other arithmetic, spread(): jax.ops.segment_sum(partial_value, row_list, num_segments=count * front_w...  31.1 us
    ppermute x4, waiting for transfers between devices, partner(): return lax.ppermute(block, axis, route)  13.3 us
  transfers between devices with their start and end apart: 8, of which 8 were waited for; matrix products, arithmetic and copies ran while one was open for 0% of the time, Pallas kernels for 0%

commit v1 on v0

--- a/solution.py
+++ b/solution.py
@@ -2,6 +2,25 @@
 import jax.numpy as jnp
 from jax import lax
 from jax.sharding import PartitionSpec as P
+
+
+def gather_around(array, axis, dim):
+    size, here, rows = (lax.axis_size(axis), lax.axis_index(axis), array.shape[dim])
+    upward = [(i, (i + 1) % size) for i in range(size)]
+    left = [(i, (i - 1) % size) for i in range(size)]
+    out = jnp.zeros((*array.shape[:dim], size * rows, *array.shape[dim + 1 :]), array.dtype)
+    out = lax.dynamic_update_slice_in_dim(out, array, here * rows, axis=dim)
+    from_left = from_right = array
+    half = size // 2
+    for step in range(1, half + 1):
+        from_left = lax.ppermute(from_left, axis, upward)
+        out = lax.dynamic_update_slice_in_dim(out, from_left, (here - step) % size * rows, axis=dim)
+        if step < size - half:
+            from_right = lax.ppermute(from_right, axis, left)
+            out = lax.dynamic_update_slice_in_dim(
+                out, from_right, (here + step) % size * rows, axis=dim
+            )
+    return out
 
 
 def partner(block, axis, stride):
@@ -24,9 +43,7 @@
     def apply_inverse(inverse, right_side):
         rounded = right_side.astype(jnp.bfloat16)
         return jnp.dot(
-            inverse,
-            lax.all_gather(rounded, "front", axis=0, tiled=True),
-            preferred_element_type=jnp.float32,
+            inverse, gather_around(rounded, "front", 0), preferred_element_type=jnp.float32
         )
 
     def spread(off_block, solution, row_list, count):

time: 522 us -> 693 us (1.33); the launches traced: 521 us -> 684 us
  starting transfers between devices: 8.32 us -> 200 us
  blocking collectives: 118 us -> 0 us
  waiting for transfers between devices: 332 us -> 421 us
    ppermute x0 -> x75, starting transfers between devices: none -> 192 us  [the longest x35 184 us: gather_around(): from_right = lax.ppermute(from_right, axis, left)]
    all_gather x5 -> x0, blocking collectives: 118 us -> none  [apply_inverse(): lax.all_gather(rounded, 'front', axis=0, tiled=True)]
    ppermute x0 -> x75, waiting for transfers between devices: none -> 98.1 us  [the longest x40 94.6 us: gather_around(): from_left = lax.ppermute(from_left, axis, upward)]
    reduce_scatter x4, waiting for transfers between devices: 319 us -> 309 us  [spread(): lax.psum_scatter(dense_rows, 'front', scatter_dimension=1, tiled=True)]
  transfers between devices with their start and end apart: 8 -> 83, of which waited for: 8 -> 55; matrix products, arithmetic and copies ran while one was open for 0% -> 0% of each run, Pallas kernels for 0% -> 0%
where the time goes in v1:
time: 693 us; the launch traced here: 684 us
  waiting for transfers between devices  421 us (61%)
  starting transfers between devices  200 us (29%)
  other arithmetic  40 us (6%)
  between operations  14.6 us (2%)
    reduce_scatter x4, waiting for transfers between devices, spread(): lax.psum_scatter(dense_rows, 'front', scatter_dimension=1, tiled=True)  309 us
    ppermute x35, starting transfers between devices, gather_around(): from_right = lax.ppermute(from_right, axis, left)  184 us
    ppermute x40, waiting for transfers between devices, gather_around(): from_left = lax.ppermute(from_left, axis, upward)  94.6 us
    scatter-add x4, other arithmetic, spread(): jax.ops.segment_sum(partial_value, row_list, num_segments=count * front_w...  31.1 us
    ppermute x4, waiting for transfers between devices, partner(): return lax.ppermute(block, axis, route)  14.2 us
  transfers between devices with their start and end apart: 83, of which 55 were waited for; matrix products, arithmetic and copies ran while one was open for 0% of the time, Pallas kernels for 0%

profile of v1, /device:TPU:32, one launch (start us, length us, event | category | flops | bytes accessed | tf_op | source)
XLA Modules:
  0.0 684.2 jit_solution(6425564555205140837)
XLA Ops:
  9.9 3.8 collective-permute-start.1
  13.6 1.9 collective-permute-done
  15.5 5.3 collective-permute-start.3
  20.9 1.9 collective-permute-done.2
  22.8 5.3 collective-permute-start.5
  28.1 1.9 collective-permute-done.4
  30.0 5.3 collective-permute-start.7
  35.4 1.9 collective-permute-done.6
  37.2 5.3 collective-permute-start.9
  42.6 1.9 collective-permute-done.8
  44.5 5.4 collective-permute-start.11
  51.7 5.4 collective-permute-start.13
  59.1 7.2 %collective-permute-done.14 = bf16[64,256]{1,0:T(8,128)(2,1)S(1)} collective-permute-done((bf16[64,256]{1,0:T(8,128)(2,1)S(1)}, bf16[64,256]{1,0:T(8,128)(2,1)S(1)}, u32[]{:S(2)}, u32[]{:S(2)}) %collective-permute-start.14) | collective-permute-done | bytes 32800 | tf_op jit(solution)/shard_map/ppermute | solution.py:16
  68.2 8.7 %scatter_custom_fusion = f32[4096,256]{1,0:T(8,128)} fusion(s32[1024]{0:T(1024)} %bitcast.89, f32[1024,256]{1,0:T(8,128)} %copy.10, f32[]{:T(128)} %constant.289.clone.1), kind=kCustom, calls=%fused_computation.4 | custom fusion | flops 262144 | bytes 4194816 | tf_op jit(solution)/shard_map/scatter-add | solution.py:53
  77.0 80.3 %reduce-scatter.5.cloned.1.call-done = f32[4,64,256]{2,1,0:T(8,128)} async-done(((f32[4,1024,256]{2,1,0:T(8,128)}), f32[4,64,256]{2,1,0:T(8,128)}) %reduce-scatter.5.cloned.1.call-update) | async-done | bytes 262160 | tf_op jit(solution)/shard_map/reduce_scatter | solution.py:55
  163.1 4.3 collective-permute-start.17
  168.9 5.6 collective-permute-start.19
  176.2 5.6 collective-permute-start.21
  183.4 5.6 collective-permute-start.23
  190.6 5.6 collective-permute-start.25
  197.9 5.6 collective-permute-start.27
  205.1 5.6 collective-permute-start.29
  212.4 6.9 %collective-permute-done.30 = bf16[64,256]{1,0:T(8,128)(2,1)S(1)} collective-permute-done((bf16[64,256]{1,0:T(8,128)(2,1)S(1)}, bf16[64,256]{1,0:T(8,128)(2,1)S(1)}, u32[]{:S(2)}, u32[]{:S(2)}) %collective-permute-start.30) | collective-permute-done | bytes 32800 | tf_op jit(solution)/shard_map/ppermute | solution.py:16
  220.8 7.8 %scatter_custom_fusion.1 = f32[3072,256]{1,0:T(8,128)} fusion(s32[1024]{0:T(1024)S(1)} %bitcast.88, f32[1024,256]{1,0:T(8,128)S(1)} %fusion.15, f32[]{:T(128)} %constant.289.clone.1), kind=kCustom, calls=%fused_computation.6 | custom fusion | flops 262144 | bytes 3145732 | tf_op jit(solution)/shard_map/scatter-add | solution.py:53
  228.7 77.4 %reduce-scatter.7.cloned.1.call-done = f32[3,64,256]{2,1,0:T(8,128)} async-done(((f32[3,1024,256]{2,1,0:T(8,128)}), f32[3,64,256]{2,1,0:T(8,128)}) %reduce-scatter.7.cloned.1.call-update) | async-done | bytes 196624 | tf_op jit(solution)/shard_map/reduce_scatter | solution.py:55
  307.6 5.2 collective-permute-done.31
  314.9 4.2 collective-permute-start.33
  319.1 1.9 collective-permute-done.32
  321.0 5.4 collective-permute-start.35
  328.3 5.4 collective-permute-start.37
  333.7 2.1 collective-permute-done.36
  336.0 5.4 collective-permute-start.39
  343.2 5.4 collective-permute-start.41
  350.5 5.4 collective-permute-start.43
  357.7 5.4 collective-permute-start.45
  365.0 7.2 %collective-permute-done.46 = bf16[64,256]{1,0:T(8,128)(2,1)S(1)} collective-permute-done((bf16[64,256]{1,0:T(8,128)(2,1)S(1)}, bf16[64,256]{1,0:T(8,128)(2,1)S(1)}, u32[]{:S(2)}, u32[]{:S(2)}) %collective-permute-start.46) | collective-permute-done | bytes 32800 | tf_op jit(solution)/shard_map/ppermute | solution.py:16
  373.6 7.4 %scatter_custom_fusion.2 = f32[2048,256]{1,0:T(8,128)} fusion(s32[1024]{0:T(1024)S(1)} %bitcast.87, f32[1024,256]{1,0:T(8,128)S(1)} %fusion.11, f32[]{:T(128)} %constant.289.clone.1), kind=kCustom, calls=%fused_computation.10 | custom fusion | flops 262144 | bytes 2097156 | tf_op jit(solution)/shard_map/scatter-add | solution.py:53
  381.1 76.1 %reduce-scatter.9.cloned.1.call-done = f32[2,64,256]{2,1,0:T(8,128)} async-done(((f32[2,1024,256]{2,1,0:T(8,128)}), f32[2,64,256]{2,1,0:T(8,128)}) %reduce-scatter.9.cloned.1.call-update) | async-done | bytes 131088 | tf_op jit(solution)/shard_map/reduce_scatter | solution.py:55
  458.2 2.6 collective-permute-start.47
  460.8 3.8 collective-permute-done.47
  466.7 4.2 collective-permute-start.49
  470.9 1.9 collective-permute-done.48
  473.1 5.4 collective-permute-start.51
  480.3 5.4 collective-permute-start.53
  485.7 2.0 collective-permute-done.52
  487.7 5.4 collective-permute-start.55
  495.0 5.4 collective-permute-start.57
  502.2 5.4 collective-permute-start.59
  509.4 5.4 collective-permute-start.61
  517.1 7.2 %collective-permute-done.62 = bf16[64,256]{1,0:T(8,128)(2,1)S(1)} collective-permute-done((bf16[64,256]{1,0:T(8,128)(2,1)S(1)}, bf16[64,256]{1,0:T(8,128)(2,1)S(1)}, u32[]{:S(2)}, u32[]{:S(2)}) %collective-permute-start.62) | collective-permute-done | bytes 32800 | tf_op jit(solution)/shard_map/ppermute | solution.py:16
  525.7 7.1 %scatter_custom_fusion.3 = f32[1024,256]{1,0:T(8,128)} fusion(s32[1024]{0:T(1024)S(1)} %bitcast.86, f32[1024,256]{1,0:T(8,128)S(1)} %fusion.8, f32[]{:T(128)} %constant.289.clone.1), kind=kCustom, calls=%fused_computation.12 | custom fusion | flops 262144 | bytes 1048580 | tf_op jit(solution)/shard_map/scatter-add | solution.py:53
  532.8 75.4 %reduce-scatter.11.cloned.1.call-done = f32[1,64,256]{2,1,0:T(8,128)} async-done(((f32[1,1024,256]{2,1,0:T(8,128)}), f32[1,64,256]{2,1,0:T(8,128)}) %reduce-scatter.11.cloned.1.call-update) | async-done | bytes 65552 | tf_op jit(solution)/shard_map/reduce_scatter | solution.py:55
  609.1 4.9 collective-permute-start.63
  614.0 3.4 collective-permute-done.63
  619.6 4.2 collective-permute-start.65
  623.8 1.9 collective-permute-done.64
  625.7 5.4 collective-permute-start.67
  632.9 5.4 collective-permute-start.69
  638.3 2.1 collective-permute-done.68
  640.4 5.4 collective-permute-start.71
  647.7 5.4 collective-permute-start.73
  654.9 5.6 collective-permute-start.75
  662.1 5.6 collective-permute-start.77
  669.4 7.2 %collective-permute-done.78 = bf16[64,256]{1,0:T(8,128)(2,1)S(1)} collective-permute-done((bf16[64,256]{1,0:T(8,128)(2,1)S(1)}, bf16[64,256]{1,0:T(8,128)(2,1)S(1)}, u32[]{:S(2)}, u32[]{:S(2)}) %collective-permute-start.78) | collective-permute-done | bytes 32800 | tf_op jit(solution)/shard_map/ppermute | solution.py:16
  (221 shorter events, 68.2 us)
Async XLA Ops:
  7.2 150.1 %reduce-scatter.5.cloned.1.call-start = ((), (), s32[]{:S(2)}) async-start(), calls=%async_computation.4 | async-start | bytes 4456448 | tf_op jit(solution)/shard_map/reduce_scatter | solution.py:55
  8.3 7.2 %collective-permute-start = (bf16[64,256]{1,0:T(8,128)(2,1)S(1)}, bf16[64,256]{1,0:T(8,128)(2,1)S(1)}, u32[]{:S(2)}, u32[]{:S(2)}) collective-permute-start(bf16[64,256]{1,0:T(8,128)(2,1)S(1)} %get-tuple-element.11), channel_id=1, source_target_pairs={{0,1},{1,2},{2,3},{3,4},{4,5},{5,6},{6,7},{7,8},{8,9},{9,10},{10,1... | collective-permute-start | bytes 98312 | tf_op jit(solution)/shard_map/ppermute | solution.py:16
  15.5 7.2 %collective-permute-start.2 = (bf16[64,256]{1,0:T(8,128)(2,1)S(1)}, bf16[64,256]{1,0:T(8,128)(2,1)S(1)}, u32[]{:S(2)}, u32[]{:S(2)}) collective-permute-start(bf16[64,256]{1,0:T(8,128)(2,1)S(1)} %collective-permute-done), channel_id=1, source_target_pairs={{0,1},{1,2},{2,3},{3,4},{4,5},{5,6},{6,7},{7,8},{8,9},{9,10},{10,1... | collective-permute-start | bytes 98312 | tf_op jit(solution)/shard_map/ppermute | solution.py:16
  15.5 7.2 %collective-permute-start.3 = (bf16[64,256]{1,0:T(8,128)(2,1)S(1)}, bf16[64,256]{1,0:T(8,128)(2,1)S(1)}, u32[]{:S(2)}, u32[]{:S(2)}) collective-permute-start(bf16[64,256]{1,0:T(8,128)(2,1)S(1)} %collective-permute-done.1), channel_id=1, source_target_pairs={{0,15},{1,0},{2,1},{3,2},{4,3},{5,4},{6,5},{7,6},{8,7},{9,8},{10,9... | collective-permute-start | bytes 98312 | tf_op jit(solution)/shard_map/ppermute | solution.py:19
  22.8 7.2 %collective-permute-start.4 = (bf16[64,256]{1,0:T(8,128)(2,1)S(1)}, bf16[64,256]{1,0:T(8,128)(2,1)S(1)}, u32[]{:S(2)}, u32[]{:S(2)}) collective-permute-start(bf16[64,256]{1,0:T(8,128)(2,1)S(1)} %collective-permute-done.2), channel_id=1, source_target_pairs={{0,1},{1,2},{2,3},{3,4},{4,5},{5,6},{6,7},{7,8},{8,9},{9,10},{10,1... | collective-permute-start | bytes 98312 | tf_op jit(solution)/shard_map/ppermute | solution.py:16
  22.8 7.2 %collective-permute-start.5 = (bf16[64,256]{1,0:T(8,128)(2,1)S(1)}, bf16[64,256]{1,0:T(8,128)(2,1)S(1)}, u32[]{:S(2)}, u32[]{:S(2)}) collective-permute-start(bf16[64,256]{1,0:T(8,128)(2,1)S(1)} %collective-permute-done.3), channel_id=1, source_target_pairs={{0,15},{1,0},{2,1},{3,2},{4,3},{5,4},{6,5},{7,6},{8,7},{9,8},{10,9... | collective-permute-start | bytes 98312 | tf_op jit(solution)/shard_map/ppermute | solution.py:19
  30.0 7.2 %collective-permute-start.6 = (bf16[64,256]{1,0:T(8,128)(2,1)S(1)}, bf16[64,256]{1,0:T(8,128)(2,1)S(1)}, u32[]{:S(2)}, u32[]{:S(2)}) collective-permute-start(bf16[64,256]{1,0:T(8,128)(2,1)S(1)} %collective-permute-done.4), channel_id=1, source_target_pairs={{0,1},{1,2},{2,3},{3,4},{4,5},{5,6},{6,7},{7,8},{8,9},{9,10},{10,1... | collective-permute-start | bytes 98312 | tf_op jit(solution)/shard_map/ppermute | solution.py:16
  30.0 7.2 %collective-permute-start.7 = (bf16[64,256]{1,0:T(8,128)(2,1)S(1)}, bf16[64,256]{1,0:T(8,128)(2,1)S(1)}, u32[]{:S(2)}, u32[]{:S(2)}) collective-permute-start(bf16[64,256]{1,0:T(8,128)(2,1)S(1)} %collective-permute-done.5), channel_id=1, source_target_pairs={{0,15},{1,0},{2,1},{3,2},{4,3},{5,4},{6,5},{7,6},{8,7},{9,8},{10,9... | collective-permute-start | bytes 98312 | tf_op jit(solution)/shard_map/ppermute | solution.py:19
  37.2 7.2 %collective-permute-start.8 = (bf16[64,256]{1,0:T(8,128)(2,1)S(1)}, bf16[64,256]{1,0:T(8,128)(2,1)S(1)}, u32[]{:S(2)}, u32[]{:S(2)}) collective-permute-start(bf16[64,256]{1,0:T(8,128)(2,1)S(1)} %collective-permute-done.6), channel_id=1, source_target_pairs={{0,1},{1,2},{2,3},{3,4},{4,5},{5,6},{6,7},{7,8},{8,9},{9,10},{10,1... | collective-permute-start | bytes 98312 | tf_op jit(solution)/shard_map/ppermute | solution.py:16
  37.2 7.2 %collective-permute-start.9 = (bf16[64,256]{1,0:T(8,128)(2,1)S(1)}, bf16[64,256]{1,0:T(8,128)(2,1)S(1)}, u32[]{:S(2)}, u32[]{:S(2)}) collective-permute-start(bf16[64,256]{1,0:T(8,128)(2,1)S(1)} %collective-permute-done.7), channel_id=1, source_target_pairs={{0,15},{1,0},{2,1},{3,2},{4,3},{5,4},{6,5},{7,6},{8,7},{9,8},{10,9... | collective-permute-start | bytes 98312 | tf_op jit(solution)/shard_map/ppermute | solution.py:19
  44.5 7.2 %collective-permute-start.10 = (bf16[64,256]{1,0:T(8,128)(2,1)S(1)}, bf16[64,256]{1,0:T(8,128)(2,1)S(1)}, u32[]{:S(2)}, u32[]{:S(2)}) collective-permute-start(bf16[64,256]{1,0:T(8,128)(2,1)S(1)} %collective-permute-done.8), channel_id=1, source_target_pairs={{0,1},{1,2},{2,3},{3,4},{4,5},{5,6},{6,7},{7,8},{8,9},{9,10},{10,1... | collective-permute-start | bytes 98312 | tf_op jit(solution)/shard_map/ppermute | solution.py:16
  44.5 7.2 %collective-permute-start.11 = (bf16[64,256]{1,0:T(8,128)(2,1)S(1)}, bf16[64,256]{1,0:T(8,128)(2,1)S(1)}, u32[]{:S(2)}, u32[]{:S(2)}) collective-permute-start(bf16[64,256]{1,0:T(8,128)(2,1)S(1)} %collective-permute-done.9), channel_id=1, source_target_pairs={{0,15},{1,0},{2,1},{3,2},{4,3},{5,4},{6,5},{7,6},{8,7},{9,8},{10,9... | collective-permute-start | bytes 98312 | tf_op jit(solution)/shard_map/ppermute | solution.py:19
  51.7 7.2 %collective-permute-start.12 = (bf16[64,256]{1,0:T(8,128)(2,1)S(1)}, bf16[64,256]{1,0:T(8,128)(2,1)S(1)}, u32[]{:S(2)}, u32[]{:S(2)}) collective-permute-start(bf16[64,256]{1,0:T(8,128)(2,1)S(1)} %collective-permute-done.10), channel_id=1, source_target_pairs={{0,1},{1,2},{2,3},{3,4},{4,5},{5,6},{6,7},{7,8},{8,9},{9,10},{10,1... | collective-permute-start | bytes 98312 | tf_op jit(solution)/shard_map/ppermute | solution.py:16
  51.7 7.4 %collective-permute-start.13 = (bf16[64,256]{1,0:T(8,128)(2,1)S(1)}, bf16[64,256]{1,0:T(8,128)(2,1)S(1)}, u32[]{:S(2)}, u32[]{:S(2)}) collective-permute-start(bf16[64,256]{1,0:T(8,128)(2,1)S(1)} %collective-permute-done.11), channel_id=1, source_target_pairs={{0,15},{1,0},{2,1},{3,2},{4,3},{5,4},{6,5},{7,6},{8,7},{9,8},{10,9... | collective-permute-start | bytes 98312 | tf_op jit(solution)/shard_map/ppermute | solution.py:19
  58.9 7.4 %collective-permute-start.14 = (bf16[64,256]{1,0:T(8,128)(2,1)S(1)}, bf16[64,256]{1,0:T(8,128)(2,1)S(1)}, u32[]{:S(2)}, u32[]{:S(2)}) collective-permute-start(bf16[64,256]{1,0:T(8,128)(2,1)S(1)} %collective-permute-done.12), channel_id=1, source_target_pairs={{0,1},{1,2},{2,3},{3,4},{4,5},{5,6},{6,7},{7,8},{8,9},{9,10},{10,1... | collective-permute-start | bytes 98312 | tf_op jit(solution)/shard_map/ppermute | solution.py:16
  77.0 229.1 %reduce-scatter.7.cloned.1.call-start = ((), (), s32[]{:S(2)}) async-start(), calls=%async_computation.5 | async-start | bytes 3342336 | tf_op jit(solution)/shard_map/reduce_scatter | solution.py:55
  161.0 7.3 %collective-permute-start.16 = (bf16[64,256]{1,0:T(8,128)(2,1)S(1)}, bf16[64,256]{1,0:T(8,128)(2,1)S(1)}, u32[]{:S(2)}, u32[]{:S(2)}) collective-permute-start(bf16[64,256]{1,0:T(8,128)(2,1)S(1)} %get-tuple-element.9), channel_id=1, source_target_pairs={{0,1},{1,2},{2,3},{3,4},{4,5},{5,6},{6,7},{7,8},{8,9},{9,10},{10,1... | collective-permute-start | bytes 98312 | tf_op jit(solution)/shard_map/ppermute | solution.py:16
  168.3 7.2 %collective-permute-start.18 = (bf16[64,256]{1,0:T(8,128)(2,1)S(1)}, bf16[64,256]{1,0:T(8,128)(2,1)S(1)}, u32[]{:S(2)}, u32[]{:S(2)}) collective-permute-start(bf16[64,256]{1,0:T(8,128)(2,1)S(1)} %collective-permute-done.16), channel_id=1, source_target_pairs={{0,1},{1,2},{2,3},{3,4},{4,5},{5,6},{6,7},{7,8},{8,9},{9,10},{10,1... | collective-permute-start | bytes 98312 | tf_op jit(solution)/shard_map/ppermute | solution.py:16
  168.9 7.2 %collective-permute-start.19 = (bf16[64,256]{1,0:T(8,128)(2,1)S(1)}, bf16[64,256]{1,0:T(8,128)(2,1)S(1)}, u32[]{:S(2)}, u32[]{:S(2)}) collective-permute-start(bf16[64,256]{1,0:T(8,128)(2,1)S(1)} %collective-permute-done.17), channel_id=1, source_target_pairs={{0,15},{1,0},{2,1},{3,2},{4,3},{5,4},{6,5},{7,6},{8,7},{9,8},{10,9... | collective-permute-start | bytes 98312 | tf_op jit(solution)/shard_map/ppermute | solution.py:19
  175.5 7.2 %collective-permute-start.20 = (bf16[64,256]{1,0:T(8,128)(2,1)S(1)}, bf16[64,256]{1,0:T(8,128)(2,1)S(1)}, u32[]{:S(2)}, u32[]{:S(2)}) collective-permute-start(bf16[64,256]{1,0:T(8,128)(2,1)S(1)} %collective-permute-done.18), channel_id=1, source_target_pairs={{0,1},{1,2},{2,3},{3,4},{4,5},{5,6},{6,7},{7,8},{8,9},{9,10},{10,1... | collective-permute-start | bytes 98312 | tf_op jit(solution)/shard_map/ppermute | solution.py:16
  176.2 7.2 %collective-permute-start.21 = (bf16[64,256]{1,0:T(8,128)(2,1)S(1)}, bf16[64,256]{1,0:T(8,128)(2,1)S(1)}, u32[]{:S(2)}, u32[]{:S(2)}) collective-permute-start(bf16[64,256]{1,0:T(8,128)(2,1)S(1)} %collective-permute-done.19), channel_id=1, source_target_pairs={{0,15},{1,0},{2,1},{3,2},{4,3},{5,4},{6,5},{7,6},{8,7},{9,8},{10,9... | collective-permute-start | bytes 98312 | tf_op jit(solution)/shard_map/ppermute | solution.py:19
  182.7 7.2 %collective-permute-start.22 = (bf16[64,256]{1,0:T(8,128)(2,1)S(1)}, bf16[64,256]{1,0:T(8,128)(2,1)S(1)}, u32[]{:S(2)}, u32[]{:S(2)}) collective-permute-start(bf16[64,256]{1,0:T(8,128)(2,1)S(1)} %collective-permute-done.20), channel_id=1, source_target_pairs={{0,1},{1,2},{2,3},{3,4},{4,5},{5,6},{6,7},{7,8},{8,9},{9,10},{10,1... | collective-permute-start | bytes 98312 | tf_op jit(solution)/shard_map/ppermute | solution.py:16
  183.4 7.2 %collective-permute-start.23 = (bf16[64,256]{1,0:T(8,128)(2,1)S(1)}, bf16[64,256]{1,0:T(8,128)(2,1)S(1)}, u32[]{:S(2)}, u32[]{:S(2)}) collective-permute-start(bf16[64,256]{1,0:T(8,128)(2,1)S(1)} %collective-permute-done.21), channel_id=1, source_target_pairs={{0,15},{1,0},{2,1},{3,2},{4,3},{5,4},{6,5},{7,6},{8,7},{9,8},{10,9... | collective-permute-start | bytes 98312 | tf_op jit(solution)/shard_map/ppermute | solution.py:19
  190.0 7.2 %collective-permute-start.24 = (bf16[64,256]{1,0:T(8,128)(2,1)S(1)}, bf16[64,256]{1,0:T(8,128)(2,1)S(1)}, u32[]{:S(2)}, u32[]{:S(2)}) collective-permute-start(bf16[64,256]{1,0:T(8,128)(2,1)S(1)} %collective-permute-done.22), channel_id=1, source_target_pairs={{0,1},{1,2},{2,3},{3,4},{4,5},{5,6},{6,7},{7,8},{8,9},{9,10},{10,1... | collective-permute-start | bytes 98312 | tf_op jit(solution)/shard_map/ppermute | solution.py:16
  190.6 7.2 %collective-permute-start.25 = (bf16[64,256]{1,0:T(8,128)(2,1)S(1)}, bf16[64,256]{1,0:T(8,128)(2,1)S(1)}, u32[]{:S(2)}, u32[]{:S(2)}) collective-permute-start(bf16[64,256]{1,0:T(8,128)(2,1)S(1)} %collective-permute-done.23), channel_id=1, source_target_pairs={{0,15},{1,0},{2,1},{3,2},{4,3},{5,4},{6,5},{7,6},{8,7},{9,8},{10,9... | collective-permute-start | bytes 98312 | tf_op jit(solution)/shard_map/ppermute | solution.py:19
  197.2 7.6 %collective-permute-start.26 = (bf16[64,256]{1,0:T(8,128)(2,1)S(1)}, bf16[64,256]{1,0:T(8,128)(2,1)S(1)}, u32[]{:S(2)}, u32[]{:S(2)}) collective-permute-start(bf16[64,256]{1,0:T(8,128)(2,1)S(1)} %collective-permute-done.24), channel_id=1, source_target_pairs={{0,1},{1,2},{2,3},{3,4},{4,5},{5,6},{6,7},{7,8},{8,9},{9,10},{10,1... | collective-permute-start | bytes 98312 | tf_op jit(solution)/shard_map/ppermute | solution.py:16
  197.9 7.2 %collective-permute-start.27 = (bf16[64,256]{1,0:T(8,128)(2,1)S(1)}, bf16[64,256]{1,0:T(8,128)(2,1)S(1)}, u32[]{:S(2)}, u32[]{:S(2)}) collective-permute-start(bf16[64,256]{1,0:T(8,128)(2,1)S(1)} %collective-permute-done.25), channel_id=1, source_target_pairs={{0,15},{1,0},{2,1},{3,2},{4,3},{5,4},{6,5},{7,6},{8,7},{9,8},{10,9... | collective-permute-start | bytes 98312 | tf_op jit(solution)/shard_map/ppermute | solution.py:19
  204.8 7.2 %collective-permute-start.28 = (bf16[64,256]{1,0:T(8,128)(2,1)S(1)}, bf16[64,256]{1,0:T(8,128)(2,1)S(1)}, u32[]{:S(2)}, u32[]{:S(2)}) collective-permute-start(bf16[64,256]{1,0:T(8,128)(2,1)S(1)} %collective-permute-done.26), channel_id=1, source_target_pairs={{0,1},{1,2},{2,3},{3,4},{4,5},{5,6},{6,7},{7,8},{8,9},{9,10},{10,1... | collective-permute-start | bytes 98312 | tf_op jit(solution)/shard_map/ppermute | solution.py:16
  205.1 7.2 %collective-permute-start.29 = (bf16[64,256]{1,0:T(8,128)(2,1)S(1)}, bf16[64,256]{1,0:T(8,128)(2,1)S(1)}, u32[]{:S(2)}, u32[]{:S(2)}) collective-permute-start(bf16[64,256]{1,0:T(8,128)(2,1)S(1)} %collective-permute-done.27), channel_id=1, source_target_pairs={{0,15},{1,0},{2,1},{3,2},{4,3},{5,4},{6,5},{7,6},{8,7},{9,8},{10,9... | collective-permute-start | bytes 98312 | tf_op jit(solution)/shard_map/ppermute | solution.py:19
  212.1 7.2 %collective-permute-start.30 = (bf16[64,256]{1,0:T(8,128)(2,1)S(1)}, bf16[64,256]{1,0:T(8,128)(2,1)S(1)}, u32[]{:S(2)}, u32[]{:S(2)}) collective-permute-start(bf16[64,256]{1,0:T(8,128)(2,1)S(1)} %collective-permute-done.28), channel_id=1, source_target_pairs={{0,1},{1,2},{2,3},{3,4},{4,5},{5,6},{6,7},{7,8},{8,9},{9,10},{10,1... | collective-permute-start | bytes 98312 | tf_op jit(solution)/shard_map/ppermute | solution.py:16
  228.6 228.6 %reduce-scatter.9.cloned.1.call-start = ((), (), s32[]{:S(2)}) async-start(), calls=%async_computation.6 | async-start | bytes 2228224 | tf_op jit(solution)/shard_map/reduce_scatter | solution.py:55
  313.7 7.3 %collective-permute-start.32 = (bf16[64,256]{1,0:T(8,128)(2,1)S(1)}, bf16[64,256]{1,0:T(8,128)(2,1)S(1)}, u32[]{:S(2)}, u32[]{:S(2)}) collective-permute-start(bf16[64,256]{1,0:T(8,128)(2,1)S(1)} %get-tuple-element.7), channel_id=1, source_target_pairs={{0,1},{1,2},{2,3},{3,4},{4,5},{5,6},{6,7},{7,8},{8,9},{9,10},{10,1... | collective-permute-start | bytes 98312 | tf_op jit(solution)/shard_map/ppermute | solution.py:16
  321.0 7.2 %collective-permute-start.34 = (bf16[64,256]{1,0:T(8,128)(2,1)S(1)}, bf16[64,256]{1,0:T(8,128)(2,1)S(1)}, u32[]{:S(2)}, u32[]{:S(2)}) collective-permute-start(bf16[64,256]{1,0:T(8,128)(2,1)S(1)} %collective-permute-done.32), channel_id=1, source_target_pairs={{0,1},{1,2},{2,3},{3,4},{4,5},{5,6},{6,7},{7,8},{8,9},{9,10},{10,1... | collective-permute-start | bytes 98312 | tf_op jit(solution)/shard_map/ppermute | solution.py:16
  321.0 7.2 %collective-permute-start.35 = (bf16[64,256]{1,0:T(8,128)(2,1)S(1)}, bf16[64,256]{1,0:T(8,128)(2,1)S(1)}, u32[]{:S(2)}, u32[]{:S(2)}) collective-permute-start(bf16[64,256]{1,0:T(8,128)(2,1)S(1)} %collective-permute-done.33), channel_id=1, source_target_pairs={{0,15},{1,0},{2,1},{3,2},{4,3},{5,4},{6,5},{7,6},{8,7},{9,8},{10,9... | collective-permute-start | bytes 98312 | tf_op jit(solution)/shard_map/ppermute | solution.py:19
  328.3 7.6 %collective-permute-start.36 = (bf16[64,256]{1,0:T(8,128)(2,1)S(1)}, bf16[64,256]{1,0:T(8,128)(2,1)S(1)}, u32[]{:S(2)}, u32[]{:S(2)}) collective-permute-start(bf16[64,256]{1,0:T(8,128)(2,1)S(1)} %collective-permute-done.34), channel_id=1, source_target_pairs={{0,1},{1,2},{2,3},{3,4},{4,5},{5,6},{6,7},{7,8},{8,9},{9,10},{10,1... | collective-permute-start | bytes 98312 | tf_op jit(solution)/shard_map/ppermute | solution.py:16
  328.3 7.7 %collective-permute-start.37 = (bf16[64,256]{1,0:T(8,128)(2,1)S(1)}, bf16[64,256]{1,0:T(8,128)(2,1)S(1)}, u32[]{:S(2)}, u32[]{:S(2)}) collective-permute-start(bf16[64,256]{1,0:T(8,128)(2,1)S(1)} %collective-permute-done.35), channel_id=1, source_target_pairs={{0,15},{1,0},{2,1},{3,2},{4,3},{5,4},{6,5},{7,6},{8,7},{9,8},{10,9... | collective-permute-start | bytes 98312 | tf_op jit(solution)/shard_map/ppermute | solution.py:19
  335.8 7.4 %collective-permute-start.38 = (bf16[64,256]{1,0:T(8,128)(2,1)S(1)}, bf16[64,256]{1,0:T(8,128)(2,1)S(1)}, u32[]{:S(2)}, u32[]{:S(2)}) collective-permute-start(bf16[64,256]{1,0:T(8,128)(2,1)S(1)} %collective-permute-done.36), channel_id=1, source_target_pairs={{0,1},{1,2},{2,3},{3,4},{4,5},{5,6},{6,7},{7,8},{8,9},{9,10},{10,1... | collective-permute-start | bytes 98312 | tf_op jit(solution)/shard_map/ppermute | solution.py:16
  343.2 7.2 %collective-permute-start.40 = (bf16[64,256]{1,0:T(8,128)(2,1)S(1)}, bf16[64,256]{1,0:T(8,128)(2,1)S(1)}, u32[]{:S(2)}, u32[]{:S(2)}) collective-permute-start(bf16[64,256]{1,0:T(8,128)(2,1)S(1)} %collective-permute-done.38), channel_id=1, source_target_pairs={{0,1},{1,2},{2,3},{3,4},{4,5},{5,6},{6,7},{7,8},{8,9},{9,10},{10,1... | collective-permute-start | bytes 98312 | tf_op jit(solution)/shard_map/ppermute | solution.py:16
  343.2 7.2 %collective-permute-start.41 = (bf16[64,256]{1,0:T(8,128)(2,1)S(1)}, bf16[64,256]{1,0:T(8,128)(2,1)S(1)}, u32[]{:S(2)}, u32[]{:S(2)}) collective-permute-start(bf16[64,256]{1,0:T(8,128)(2,1)S(1)} %collective-permute-done.39), channel_id=1, source_target_pairs={{0,15},{1,0},{2,1},{3,2},{4,3},{5,4},{6,5},{7,6},{8,7},{9,8},{10,9... | collective-permute-start | bytes 98312 | tf_op jit(solution)/shard_map/ppermute | solution.py:19
  350.5 7.2 %collective-permute-start.42 = (bf16[64,256]{1,0:T(8,128)(2,1)S(1)}, bf16[64,256]{1,0:T(8,128)(2,1)S(1)}, u32[]{:S(2)}, u32[]{:S(2)}) collective-permute-start(bf16[64,256]{1,0:T(8,128)(2,1)S(1)} %collective-permute-done.40), channel_id=1, source_target_pairs={{0,1},{1,2},{2,3},{3,4},{4,5},{5,6},{6,7},{7,8},{8,9},{9,10},{10,1... | collective-permute-start | bytes 98312 | tf_op jit(solution)/shard_map/ppermute | solution.py:16
  357.7 7.2 %collective-permute-start.44 = (bf16[64,256]{1,0:T(8,128)(2,1)S(1)}, bf16[64,256]{1,0:T(8,128)(2,1)S(1)}, u32[]{:S(2)}, u32[]{:S(2)}) collective-permute-start(bf16[64,256]{1,0:T(8,128)(2,1)S(1)} %collective-permute-done.42), channel_id=1, source_target_pairs={{0,1},{1,2},{2,3},{3,4},{4,5},{5,6},{6,7},{7,8},{8,9},{9,10},{10,1... | collective-permute-start | bytes 98312 | tf_op jit(solution)/shard_map/ppermute | solution.py:16
  364.9 7.2 %collective-permute-start.46 = (bf16[64,256]{1,0:T(8,128)(2,1)S(1)}, bf16[64,256]{1,0:T(8,128)(2,1)S(1)}, u32[]{:S(2)}, u32[]{:S(2)}) collective-permute-start(bf16[64,256]{1,0:T(8,128)(2,1)S(1)} %collective-permute-done.44), channel_id=1, source_target_pairs={{0,1},{1,2},{2,3},{3,4},{4,5},{5,6},{6,7},{7,8},{8,9},{9,10},{10,1... | collective-permute-start | bytes 98312 | tf_op jit(solution)/shard_map/ppermute | solution.py:16
  381.1 227.1 %reduce-scatter.11.cloned.1.call-start = ((), (), s32[]{:S(2)}) async-start(), calls=%async_computation.7 | async-start | bytes 1114112 | tf_op jit(solution)/shard_map/reduce_scatter | solution.py:55
  465.5 7.3 %collective-permute-start.48 = (bf16[64,256]{1,0:T(8,128)(2,1)S(1)}, bf16[64,256]{1,0:T(8,128)(2,1)S(1)}, u32[]{:S(2)}, u32[]{:S(2)}) collective-permute-start(bf16[64,256]{1,0:T(8,128)(2,1)S(1)} %get-tuple-element.5), channel_id=1, source_target_pairs={{0,1},{1,2},{2,3},{3,4},{4,5},{5,6},{6,7},{7,8},{8,9},{9,10},{10,1... | collective-permute-start | bytes 98312 | tf_op jit(solution)/shard_map/ppermute | solution.py:16
  472.8 7.4 %collective-permute-start.50 = (bf16[64,256]{1,0:T(8,128)(2,1)S(1)}, bf16[64,256]{1,0:T(8,128)(2,1)S(1)}, u32[]{:S(2)}, u32[]{:S(2)}) collective-permute-start(bf16[64,256]{1,0:T(8,128)(2,1)S(1)} %collective-permute-done.48), channel_id=1, source_target_pairs={{0,1},{1,2},{2,3},{3,4},{4,5},{5,6},{6,7},{7,8},{8,9},{9,10},{10,1... | collective-permute-start | bytes 98312 | tf_op jit(solution)/shard_map/ppermute | solution.py:16
  480.3 7.5 %collective-permute-start.52 = (bf16[64,256]{1,0:T(8,128)(2,1)S(1)}, bf16[64,256]{1,0:T(8,128)(2,1)S(1)}, u32[]{:S(2)}, u32[]{:S(2)}) collective-permute-start(bf16[64,256]{1,0:T(8,128)(2,1)S(1)} %collective-permute-done.50), channel_id=1, source_target_pairs={{0,1},{1,2},{2,3},{3,4},{4,5},{5,6},{6,7},{7,8},{8,9},{9,10},{10,1... | collective-permute-start | bytes 98312 | tf_op jit(solution)/shard_map/ppermute | solution.py:16
  480.3 7.5 %collective-permute-start.53 = (bf16[64,256]{1,0:T(8,128)(2,1)S(1)}, bf16[64,256]{1,0:T(8,128)(2,1)S(1)}, u32[]{:S(2)}, u32[]{:S(2)}) collective-permute-start(bf16[64,256]{1,0:T(8,128)(2,1)S(1)} %collective-permute-done.51), channel_id=1, source_target_pairs={{0,15},{1,0},{2,1},{3,2},{4,3},{5,4},{6,5},{7,6},{8,7},{9,8},{10,9... | collective-permute-start | bytes 98312 | tf_op jit(solution)/shard_map/ppermute | solution.py:19
  487.7 7.2 %collective-permute-start.54 = (bf16[64,256]{1,0:T(8,128)(2,1)S(1)}, bf16[64,256]{1,0:T(8,128)(2,1)S(1)}, u32[]{:S(2)}, u32[]{:S(2)}) collective-permute-start(bf16[64,256]{1,0:T(8,128)(2,1)S(1)} %collective-permute-done.52), channel_id=1, source_target_pairs={{0,1},{1,2},{2,3},{3,4},{4,5},{5,6},{6,7},{7,8},{8,9},{9,10},{10,1... | collective-permute-start | bytes 98312 | tf_op jit(solution)/shard_map/ppermute | solution.py:16
  487.7 7.2 %collective-permute-start.55 = (bf16[64,256]{1,0:T(8,128)(2,1)S(1)}, bf16[64,256]{1,0:T(8,128)(2,1)S(1)}, u32[]{:S(2)}, u32[]{:S(2)}) collective-permute-start(bf16[64,256]{1,0:T(8,128)(2,1)S(1)} %collective-permute-done.53), channel_id=1, source_target_pairs={{0,15},{1,0},{2,1},{3,2},{4,3},{5,4},{6,5},{7,6},{8,7},{9,8},{10,9... | collective-permute-start | bytes 98312 | tf_op jit(solution)/shard_map/ppermute | solution.py:19
  495.0 7.2 %collective-permute-start.56 = (bf16[64,256]{1,0:T(8,128)(2,1)S(1)}, bf16[64,256]{1,0:T(8,128)(2,1)S(1)}, u32[]{:S(2)}, u32[]{:S(2)}) collective-permute-start(bf16[64,256]{1,0:T(8,128)(2,1)S(1)} %collective-permute-done.54), channel_id=1, source_target_pairs={{0,1},{1,2},{2,3},{3,4},{4,5},{5,6},{6,7},{7,8},{8,9},{9,10},{10,1... | collective-permute-start | bytes 98312 | tf_op jit(solution)/shard_map/ppermute | solution.py:16
  502.2 7.2 %collective-permute-start.58 = (bf16[64,256]{1,0:T(8,128)(2,1)S(1)}, bf16[64,256]{1,0:T(8,128)(2,1)S(1)}, u32[]{:S(2)}, u32[]{:S(2)}) collective-permute-start(bf16[64,256]{1,0:T(8,128)(2,1)S(1)} %collective-permute-done.56), channel_id=1, source_target_pairs={{0,1},{1,2},{2,3},{3,4},{4,5},{5,6},{6,7},{7,8},{8,9},{9,10},{10,1... | collective-permute-start | bytes 98312 | tf_op jit(solution)/shard_map/ppermute | solution.py:16
  509.4 7.2 %collective-permute-start.60 = (bf16[64,256]{1,0:T(8,128)(2,1)S(1)}, bf16[64,256]{1,0:T(8,128)(2,1)S(1)}, u32[]{:S(2)}, u32[]{:S(2)}) collective-permute-start(bf16[64,256]{1,0:T(8,128)(2,1)S(1)} %collective-permute-done.58), channel_id=1, source_target_pairs={{0,1},{1,2},{2,3},{3,4},{4,5},{5,6},{6,7},{7,8},{8,9},{9,10},{10,1... | collective-permute-start | bytes 98312 | tf_op jit(solution)/shard_map/ppermute | solution.py:16
  509.4 7.6 %collective-permute-start.61 = (bf16[64,256]{1,0:T(8,128)(2,1)S(1)}, bf16[64,256]{1,0:T(8,128)(2,1)S(1)}, u32[]{:S(2)}, u32[]{:S(2)}) collective-permute-start(bf16[64,256]{1,0:T(8,128)(2,1)S(1)} %collective-permute-done.59), channel_id=1, source_target_pairs={{0,15},{1,0},{2,1},{3,2},{4,3},{5,4},{6,5},{7,6},{8,7},{9,8},{10,9... | collective-permute-start | bytes 98312 | tf_op jit(solution)/shard_map/ppermute | solution.py:19
  516.7 7.6 %collective-permute-start.62 = (bf16[64,256]{1,0:T(8,128)(2,1)S(1)}, bf16[64,256]{1,0:T(8,128)(2,1)S(1)}, u32[]{:S(2)}, u32[]{:S(2)}) collective-permute-start(bf16[64,256]{1,0:T(8,128)(2,1)S(1)} %collective-permute-done.60), channel_id=1, source_target_pairs={{0,1},{1,2},{2,3},{3,4},{4,5},{5,6},{6,7},{7,8},{8,9},{9,10},{10,1... | collective-permute-start | bytes 98312 | tf_op jit(solution)/shard_map/ppermute | solution.py:16
  609.1 8.4 %collective-permute-start.63 = (f32[1,64,256]{2,1,0:T(8,128)S(1)}, f32[1,64,256]{2,1,0:T(8,128)S(1)}, u32[]{:S(2)}, u32[]{:S(2)}) collective-permute-start(f32[1,64,256]{2,1,0:T(8,128)S(1)} %slice_add_fusion.2), channel_id=1, source_target_pairs={{0,128},{128,0},{16,144},{144,16},{32,160},{160,32},{48,176},{176,... | collective-permute-start | bytes 196616 | tf_op jit(solution)/shard_map/ppermute | solution.py:33
  618.4 7.3 %collective-permute-start.64 = (bf16[64,256]{1,0:T(8,128)(2,1)S(1)}, bf16[64,256]{1,0:T(8,128)(2,1)S(1)}, u32[]{:S(2)}, u32[]{:S(2)}) collective-permute-start(bf16[64,256]{1,0:T(8,128)(2,1)S(1)} %get-tuple-element.3), channel_id=1, source_target_pairs={{0,1},{1,2},{2,3},{3,4},{4,5},{5,6},{6,7},{7,8},{8,9},{9,10},{10,1... | collective-permute-start | bytes 98312 | tf_op jit(solution)/shard_map/ppermute | solution.py:16
  625.7 7.2 %collective-permute-start.66 = (bf16[64,256]{1,0:T(8,128)(2,1)S(1)}, bf16[64,256]{1,0:T(8,128)(2,1)S(1)}, u32[]{:S(2)}, u32[]{:S(2)}) collective-permute-start(bf16[64,256]{1,0:T(8,128)(2,1)S(1)} %collective-permute-done.64), channel_id=1, source_target_pairs={{0,1},{1,2},{2,3},{3,4},{4,5},{5,6},{6,7},{7,8},{8,9},{9,10},{10,1... | collective-permute-start | bytes 98312 | tf_op jit(solution)/shard_map/ppermute | solution.py:16
  632.9 7.5 %collective-permute-start.68 = (bf16[64,256]{1,0:T(8,128)(2,1)S(1)}, bf16[64,256]{1,0:T(8,128)(2,1)S(1)}, u32[]{:S(2)}, u32[]{:S(2)}) collective-permute-start(bf16[64,256]{1,0:T(8,128)(2,1)S(1)} %collective-permute-done.66), channel_id=1, source_target_pairs={{0,1},{1,2},{2,3},{3,4},{4,5},{5,6},{6,7},{7,8},{8,9},{9,10},{10,1... | collective-permute-start | bytes 98312 | tf_op jit(solution)/shard_map/ppermute | solution.py:16
  632.9 7.5 %collective-permute-start.69 = (bf16[64,256]{1,0:T(8,128)(2,1)S(1)}, bf16[64,256]{1,0:T(8,128)(2,1)S(1)}, u32[]{:S(2)}, u32[]{:S(2)}) collective-permute-start(bf16[64,256]{1,0:T(8,128)(2,1)S(1)} %collective-permute-done.67), channel_id=1, source_target_pairs={{0,15},{1,0},{2,1},{3,2},{4,3},{5,4},{6,5},{7,6},{8,7},{9,8},{10,9... | collective-permute-start | bytes 98312 | tf_op jit(solution)/shard_map/ppermute | solution.py:19
  640.4 7.2 %collective-permute-start.70 = (bf16[64,256]{1,0:T(8,128)(2,1)S(1)}, bf16[64,256]{1,0:T(8,128)(2,1)S(1)}, u32[]{:S(2)}, u32[]{:S(2)}) collective-permute-start(bf16[64,256]{1,0:T(8,128)(2,1)S(1)} %collective-permute-done.68), channel_id=1, source_target_pairs={{0,1},{1,2},{2,3},{3,4},{4,5},{5,6},{6,7},{7,8},{8,9},{9,10},{10,1... | collective-permute-start | bytes 98312 | tf_op jit(solution)/shard_map/ppermute | solution.py:16
  647.6 7.2 %collective-permute-start.72 = (bf16[64,256]{1,0:T(8,128)(2,1)S(1)}, bf16[64,256]{1,0:T(8,128)(2,1)S(1)}, u32[]{:S(2)}, u32[]{:S(2)}) collective-permute-start(bf16[64,256]{1,0:T(8,128)(2,1)S(1)} %collective-permute-done.70), channel_id=1, source_target_pairs={{0,1},{1,2},{2,3},{3,4},{4,5},{5,6},{6,7},{7,8},{8,9},{9,10},{10,1... | collective-permute-start | bytes 98312 | tf_op jit(solution)/shard_map/ppermute | solution.py:16
  654.9 7.2 %collective-permute-start.74 = (bf16[64,256]{1,0:T(8,128)(2,1)S(1)}, bf16[64,256]{1,0:T(8,128)(2,1)S(1)}, u32[]{:S(2)}, u32[]{:S(2)}) collective-permute-start(bf16[64,256]{1,0:T(8,128)(2,1)S(1)} %collective-permute-done.72), channel_id=1, source_target_pairs={{0,1},{1,2},{2,3},{3,4},{4,5},{5,6},{6,7},{7,8},{8,9},{9,10},{10,1... | collective-permute-start | bytes 98312 | tf_op jit(solution)/shard_map/ppermute | solution.py:16
  662.1 7.2 %collective-permute-start.76 = (bf16[64,256]{1,0:T(8,128)(2,1)S(1)}, bf16[64,256]{1,0:T(8,128)(2,1)S(1)}, u32[]{:S(2)}, u32[]{:S(2)}) collective-permute-start(bf16[64,256]{1,0:T(8,128)(2,1)S(1)} %collective-permute-done.74), channel_id=1, source_target_pairs={{0,1},{1,2},{2,3},{3,4},{4,5},{5,6},{6,7},{7,8},{8,9},{9,10},{10,1... | collective-permute-start | bytes 98312 | tf_op jit(solution)/shard_map/ppermute | solution.py:16
  669.3 7.2 %collective-permute-start.78 = (bf16[64,256]{1,0:T(8,128)(2,1)S(1)}, bf16[64,256]{1,0:T(8,128)(2,1)S(1)}, u32[]{:S(2)}, u32[]{:S(2)}) collective-permute-start(bf16[64,256]{1,0:T(8,128)(2,1)S(1)} %collective-permute-done.76), channel_id=1, source_target_pairs={{0,1},{1,2},{2,3},{3,4},{4,5},{5,6},{6,7},{7,8},{8,9},{9,10},{10,1... | collective-permute-start | bytes 98312 | tf_op jit(solution)/shard_map/ppermute | solution.py:16
  (23 other events, 464.5 us)
Sparse Core Ops, SparseCore 0:
  77.1 80.1 reduce-scatter.4
  228.7 77.2 reduce-scatter.6
  381.2 75.9 reduce-scatter.8
  533.0 75.2 reduce-scatter.10
